TPU v7x, 32 devices: a whole 2x2x4 slice. The times are simulated.
32 devices in a mesh: pair: 8 (over z, x), blk: 4 (over y, core).
Axes of the slice: x: 2, y: 2, z: 4, core: 2. Of those that a mesh axis runs over, the one named last changes fastest.
Arguments:
- integrals: bfloat16 [32, 4, 2, 64, 4096], P(('pair', 'blk')), may hold values from -6 to 6
- density: bfloat16 [12, 16384], P(None, 'blk'), may hold values from -0.75 to 0.75
- metric: bfloat16 [512, 512], P('pair'), may hold values from -0.5 to 0.5
- nu_local: int32 [32, 4, 2], P(('pair', 'blk')), may hold values from 0 to 63
- p_index: int32 [32, 4, 2], P(('pair', 'blk')), may hold values from 0 to 7
- counts: int32 [32, 4], P(('pair', 'blk')), may hold values from 0 to 2, as said below
Outputs:
- remapped: bfloat16 [8, 4, 512, 768], P(None, 'blk', 'pair')
Inputs may be any that keep to these rules, and one draw needn't show every extreme that they name: `counts`: in every draw all panels of at least one orbital block are filled to 2.
All inputs are finite; a program needn't handle non-finite values.
Results may differ from a plain program's by a relative error of at most 0.0049.
Values may be sent and summed in bfloat16 or wider, within the bound.
A program may use at most 128 MiB of HBM per device.

v0:
```python
import jax
import jax.numpy as jnp
from jax import lax
from jax.sharding import PartitionSpec as P


def passed_along(block, axis, distance):
    devices = range(lax.axis_size(axis))
    route = [((i - distance) % len(devices), i) for i in devices]
    return lax.ppermute(block, axis, route)


def per_device(integrals, density, metric, nu_local, p_index, counts):
    cycle_size = lax.axis_size("blk")
    cycle_pos = lax.axis_index("blk")
    block_width = integrals.shape[3]
    slot_count = integrals.shape[2]
    columns = density.shape[0]
    aux_width = metric.shape[1]
    aux_blocks = aux_width // block_width
    block_data = integrals[0]
    nu_slots = nu_local[0]
    aux_slots = p_index[0]
    filled = counts[0]
    offsets = jnp.arange(block_width, dtype=jnp.int32)
    slot_ids = jnp.arange(slot_count, dtype=jnp.int32)
    stack = jnp.zeros((cycle_size * slot_count, block_width, block_width * columns), jnp.float32)
    panel_now = density
    for turn_id in range(cycle_size):
        group_id = (cycle_pos - turn_id) % cycle_size
        cube = lax.dynamic_index_in_dim(block_data, group_id, 0, keepdims=False)
        local_nu = lax.dynamic_index_in_dim(nu_slots, group_id, 0, keepdims=False)
        col_index = (local_nu * block_width)[:, None] + offsets[None, :]
        dens_cols = jnp.take(panel_now, col_index, axis=1)
        contrib = jnp.einsum("sgn,gnx->gxs", dens_cols, cube, preferred_element_type=jnp.float32)
        contrib = contrib.reshape(slot_count, block_width, block_width * columns)
        stack = lax.dynamic_update_slice_in_dim(stack, contrib, group_id * slot_count, 0)
        if turn_id + 1 < cycle_size:
            panel_now = passed_along(panel_now, "blk", 1)
    live_slots = (slot_ids[None, :] < filled[:, None]).reshape(-1)
    targets = aux_slots.reshape(-1)
    block_ids = jnp.arange(aux_blocks, dtype=jnp.int32)
    selector = jnp.where(
        (targets[:, None] == block_ids[None, :]) & live_slots[:, None], 1.0, 0.0
    ).astype(jnp.float32)
    xblocks = jnp.einsum(
        "kp,kix->pix",
        selector,
        stack,
        precision=lax.Precision.HIGHEST,
        preferred_element_type=jnp.float32,
    )
    xmatrix = xblocks.astype(jnp.bfloat16).reshape(aux_width, block_width * columns)
    whole_metric = lax.all_gather(metric, "pair", axis=0, tiled=True)
    results = lax.dot_general(
        whole_metric, xmatrix, (((0,), (0,)), ((), ())), preferred_element_type=jnp.float32
    )
    result_rows = results.astype(jnp.bfloat16).reshape(1, 1, aux_width, block_width * columns)
    return lax.all_to_all(result_rows, "pair", split_axis=2, concat_axis=0, tiled=True)


def solution(mesh):
    in_specs = (
        P(("pair", "blk"), None, None, None, None),
        P(None, "blk"),
        P("pair", None),
        P(("pair", "blk"), None, None),
        P(("pair", "blk"), None, None),
        P(("pair", "blk"), None),
    )
    out_specs = P(None, "blk", "pair", None)
    return jax.shard_map(
        per_device, mesh=mesh, in_specs=in_specs, out_specs=out_specs, check_vma=False
    )
```

profile of v0, /device:TPU:0, one launch (start us, length us, event | category | flops | bytes accessed | tf_op | source)
XLA Modules:
  0.0 124.2 jit_solution(17048398438420139386)
XLA Ops:
  0.0 0.5 collective-permute-start
  0.5 1.0 fusion.48
  1.6 1.4 %copy.34 = bf16[12,4096]{0,1:T(8,128)(2,1)S(1)} copy(bf16[12,4096]{1,0:T(8,128)(2,1)} %param.9) | data formatting | bytes 196608 | tf_op args[1]
  3.4 0.7 gather_fusion
  4.2 4.1 %fusion.7 = f32[2,4096,12]{2,1,0:T(8,128)} fusion(bf16[1,4,2,64,4096]{4,3,2,1,0:T(8,128)(2,1)} %param.8, s32[]{:T(128)S(6)} %select_n.62, bf16[2,64,12]{1,2,0:T(8,128)(2,1)S(1)} %copy.35, pred[2,64]{1,0:T(4,128)(4,1)S(1)} %get-tuple-element.17), kind=kOutput, calls=%fused_computation.13 | convolution fusion | flops 12584448 | bytes 1444996 | tf_op jit(solution)/shard_map/sgn,gnx->gxs/dot_general | solution.py:35
  8.3 5.0 %reshape.86 = f32[2,64,768]{2,1,0:T(8,128)S(1)} reshape(f32[2,4096,12]{2,1,0:T(8,128)} %fusion.7) | data formatting | bytes 786432 | tf_op jit(solution)/shard_map/reshape | solution.py:36
  13.8 32.7 %all_gather.3 = bf16[512,512]{1,0:T(8,128)(2,1)S(1)} all-gather(bf16[64,512]{1,0:T(8,128)(2,1)S(1)} %copy-done), channel_id=1, replica_groups=mesh['pair'=8,'blk'=4] {'pair'}, dimensions={0}, use_global_device_ids=true | all-gather | bytes 589824 | tf_op jit(solution)/shard_map/all_gather | solution.py:54
  46.6 0.4 copy_dynamic-update-slice_fusion.3
  47.0 0.5 copy.38
  47.5 0.7 gather_fusion.1
  48.4 4.1 %fusion.5 = f32[2,4096,12]{2,1,0:T(8,128)} fusion(bf16[1,4,2,64,4096]{4,3,2,1,0:T(8,128)(2,1)} %param.8, s32[]{:T(128)S(6)} %select_n.65, bf16[2,64,12]{1,2,0:T(8,128)(2,1)S(1)} %copy.39, pred[2,64]{1,0:T(4,128)(4,1)S(1)} %get-tuple-element.16), kind=kOutput, calls=%fused_computation.11 | convolution fusion | flops 12584448 | bytes 1444996 | tf_op jit(solution)/shard_map/sgn,gnx->gxs/dot_general | solution.py:35
  52.4 4.9 %reshape.87 = f32[2,64,768]{2,1,0:T(8,128)S(1)} reshape(f32[2,4096,12]{2,1,0:T(8,128)} %fusion.5) | data formatting | bytes 786432 | tf_op jit(solution)/shard_map/reshape | solution.py:36
  57.4 0.4 copy_dynamic-update-slice_fusion.2
  57.9 3.9 %collective-permute-done.1 = bf16[12,4096]{1,0:T(8,128)(2,1)S(1)} collective-permute-done((bf16[12,4096]{1,0:T(8,128)(2,1)S(1)}, bf16[12,4096]{1,0:T(8,128)(2,1)S(1)}, u32[]{:S(2)}, u32[]{:S(2)}) %collective-permute-start.1) | collective-permute-done | bytes 98336 | tf_op jit(solution)/shard_map/ppermute | solution.py:10
  61.8 0.5 copy.42
  62.3 0.7 gather_fusion.2
  63.1 4.1 %fusion.3 = f32[2,4096,12]{2,1,0:T(8,128)} fusion(bf16[1,4,2,64,4096]{4,3,2,1,0:T(8,128)(2,1)} %param.8, s32[]{:T(128)S(6)} %select_n.68, bf16[2,64,12]{1,2,0:T(8,128)(2,1)S(1)} %copy.43, pred[2,64]{1,0:T(4,128)(4,1)S(1)} %get-tuple-element.15), kind=kOutput, calls=%fused_computation.9 | convolution fusion | flops 12584448 | bytes 1444996 | tf_op jit(solution)/shard_map/sgn,gnx->gxs/dot_general | solution.py:35
  67.2 4.9 %reshape.88 = f32[2,64,768]{2,1,0:T(8,128)S(1)} reshape(f32[2,4096,12]{2,1,0:T(8,128)} %fusion.3) | data formatting | bytes 786432 | tf_op jit(solution)/shard_map/reshape | solution.py:36
  72.4 0.4 copy_dynamic-update-slice_fusion.1
  72.9 3.9 %collective-permute-done.2 = bf16[12,4096]{1,0:T(8,128)(2,1)S(1)} collective-permute-done((bf16[12,4096]{1,0:T(8,128)(2,1)S(1)}, bf16[12,4096]{1,0:T(8,128)(2,1)S(1)}, u32[]{:S(2)}, u32[]{:S(2)}) %collective-permute-start.2) | collective-permute-done | bytes 98336 | tf_op jit(solution)/shard_map/ppermute | solution.py:10
  76.8 0.5 copy.46
  77.3 0.7 gather_fusion.3
  78.1 4.1 %fusion.1 = f32[2,4096,12]{2,1,0:T(8,128)} fusion(bf16[1,4,2,64,4096]{4,3,2,1,0:T(8,128)(2,1)} %param.8, s32[]{:T(128)S(6)} %select_n.71, bf16[2,64,12]{1,2,0:T(8,128)(2,1)S(1)} %copy.47, pred[2,64]{1,0:T(4,128)(4,1)S(1)} %get-tuple-element.14), kind=kOutput, calls=%fused_computation.7 | convolution fusion | flops 12584448 | bytes 1444996 | tf_op jit(solution)/shard_map/sgn,gnx->gxs/dot_general | solution.py:35
  82.2 4.9 %reshape.89 = f32[2,64,768]{2,1,0:T(8,128)S(1)} reshape(f32[2,4096,12]{2,1,0:T(8,128)} %fusion.1) | data formatting | bytes 786432 | tf_op jit(solution)/shard_map/reshape | solution.py:36
  87.6 1.4 %convolution_convert_fusion.1 = bf16[8,64,768]{2,0,1:T(8,128)(2,1)S(1)} fusion(f32[8,64,768]{2,0,1:T(8,128)S(1)} %copy_dynamic-update-slice_fusion, s32[8]{0:T(128)S(1)} %eq.20, pred[8]{0:T(512)(128)(4,1)S(1)} %lt.80), kind=kOutput, calls=%fused_computation.5 | convolution fusion | flops 38142144 | bytes 2359336 | tf_op jit(solution)/shard_map/kp,kix->pix/dot_general | solution.py:46
  89.1 0.6 fusion
  89.7 1.6 %copy.51 = bf16[1,1,512,768]{3,1,0,2:T(2,128)(2,1)S(1)} copy(bf16[1,1,512,768]{2,3,1,0:T(8,128)(2,1)S(1)} %fusion) | data formatting | bytes 1572864 | tf_op jit(solution)/shard_map/reshape | solution.py:58
  91.3 0.5 broadcast.112
  91.8 5.4 %reduce.8 = bf16[512,768]{1,0:T(8,128)(2,1)S(1)} reduce(bf16[512,1,1,768]{3,2,1,0:T(2,128)(2,1)S(1)} %bitcast.45, bf16[]{:T(256)} %broadcast.112), dimensions={1,2}, to_apply=%bitcast.40.reduce_sub_computation | reduce | bytes 1572866
  97.5 24.9 %all_to_all.12 = bf16[8,2,24576]{2,1,0:T(2,128)(2,1)S(1)} all-to-all(bf16[8,2,24576]{2,1,0:T(2,128)(2,1)S(1)} %reshape.153), channel_id=1, replica_groups=mesh['pair'=8,'blk'=4] {'pair'}, dimensions={0} | all-to-all | bytes 1572864 | tf_op jit(solution)/shard_map/all_to_all | solution.py:59
  122.4 0.8 reshape.154
  123.2 1.0 copy.57
  (33 shorter events, 2.6 us)
Async XLA Ops:
  0.0 47.0 %collective-permute-start = (bf16[12,4096]{1,0:T(8,128)(2,1)}, bf16[12,4096]{1,0:T(8,128)(2,1)S(1)}, u32[]{:S(2)}, u32[]{:S(2)}) collective-permute-start(bf16[12,4096]{1,0:T(8,128)(2,1)} %param.9), channel_id=1, source_target_pairs={{3,0},{0,1},{1,2},{2,3},{7,4},{4,5},{5,6},{6,7},{11,8},{8,9},{9,10... | collective-permute-start | bytes 294920 | tf_op jit(solution)/shard_map/ppermute | solution.py:10
  8.3 5.1 %copy-start.1 = (s32[1,4,2]{1,2,0:T(2,128)S(1)}, s32[1,4,2]{1,2,0:T(2,128)}, u32[]{:S(2)}) copy-start(s32[1,4,2]{1,2,0:T(2,128)} %param.12) | copy-start | bytes 100
  8.3 5.3 %copy-start.2 = (s32[1,4]{1,0:T(1,128)S(1)}, s32[1,4]{1,0:T(1,128)}, u32[]{:S(2)}) copy-start(s32[1,4]{1,0:T(1,128)} %param.13) | copy-start | bytes 52
  8.3 5.5 %copy-start = (bf16[64,512]{1,0:T(8,128)(2,1)S(1)}, bf16[64,512]{1,0:T(8,128)(2,1)}, u32[]{:S(2)}) copy-start(bf16[64,512]{1,0:T(8,128)(2,1)} %param.10) | copy-start | bytes 196612
  57.4 4.4 %collective-permute-start.1 = (bf16[12,4096]{1,0:T(8,128)(2,1)S(1)}, bf16[12,4096]{1,0:T(8,128)(2,1)S(1)}, u32[]{:S(2)}, u32[]{:S(2)}) collective-permute-start(bf16[12,4096]{1,0:T(8,128)(2,1)S(1)} %collective-permute-done), channel_id=1, source_target_pairs={{3,0},{0,1},{1,2},{2,3},{7,4},{4,5},{5,6},{6,7},{11,8},{8,9},{9,10... | collective-permute-start | bytes 294920 | tf_op jit(solution)/shard_map/ppermute | solution.py:10
  72.2 4.6 %collective-permute-start.2 = (bf16[12,4096]{1,0:T(8,128)(2,1)S(1)}, bf16[12,4096]{1,0:T(8,128)(2,1)S(1)}, u32[]{:S(2)}, u32[]{:S(2)}) collective-permute-start(bf16[12,4096]{1,0:T(8,128)(2,1)S(1)} %collective-permute-done.1), channel_id=1, source_target_pairs={{3,0},{0,1},{1,2},{2,3},{7,4},{4,5},{5,6},{6,7},{11,8},{8,9},{9,10... | collective-permute-start | bytes 294920 | tf_op jit(solution)/shard_map/ppermute | solution.py:10
where the time goes:
time: 125 us; the launch traced here: 124 us
  blocking collectives  57.6 us (46%)
  local copies, waits for them, and re-layouts  32.6 us (26%)
  matrix products  18.4 us (15%)
  waiting for transfers between devices  7.86 us (6%)
  other arithmetic  6.87 us (5%)
    all_gather x1, blocking collectives, per_device(): whole_metric = lax.all_gather(metric, 'pair', axis=0, tiled=True)  32.7 us
    all_to_all x1, blocking collectives, per_device(): lax.all_to_all(result_rows, 'pair', split_axis=2, concat_axis=0, tiled=True)  24.9 us
    reshape x4, local copies, waits for them, and re-layouts, per_device(): contrib = contrib.reshape(slot_count, block_width, block_width * columns)  19.7 us
    dot_general x4, matrix products, per_device(): jnp.einsum('sgn,gnx->gxs', dens_cols, cube, preferred_element_type=jnp.fl...  16.4 us
    ppermute x3, waiting for transfers between devices, passed_along(): return lax.ppermute(block, axis, route)  7.86 us
    unnamed x1, other arithmetic  5.43 us
    unnamed x12, local copies, waits for them, and re-layouts  4.01 us
    gather x8, local copies, waits for them, and re-layouts, per_device(): dens_cols = jnp.take(panel_now, col_index, axis=1)  3.23 us
  transfers between devices with their start and end apart: 3, of which 2 were waited for; matrix products, arithmetic and copies ran while one was open for 12% of the time, Pallas kernels for 0%

commit v1 on v0

v1 whole, which is shorter than its diff:
```python
import functools

import jax
import jax.numpy as jnp
from jax import lax
from jax.experimental import pallas as pl
from jax.experimental.pallas import tpu as pltpu
from jax.sharding import PartitionSpec as P

MESH = pl.DeviceIdType.MESH
BF16 = jnp.bfloat16
F32 = jnp.float32


def offsets_far_first(count):
    return sorted(range(1, count), key=lambda off: -min(off, count - off))


def kernel(pairs, blks, nu_ref, p_ref, cnt_ref, ints_ref, dens_ref, metric_ref, out_ref,
           a_buf, dens_all, met_all, zbuf, xbuf, perm, ysend, lbuf,
           a_sem, dsend, drecv, msend, mrecv, ysems, yrecv, own_sem):
    q = lax.axis_index("pair")
    b = lax.axis_index("blk")
    core = lax.rem(b, 2)
    sib = b + 1 - 2 * core
    chips = blks // 2
    slots = p_ref.shape[2]
    bs = metric_ref.shape[0]
    half = bs // 2
    aux = metric_ref.shape[1]
    sig = dens_ref.shape[0]
    cols = sig * bs
    pn = aux // bs
    offs = offsets_far_first(pairs)
    slot_rows = slots * bs

    a_copies = []
    for g in range(blks):
        for k in range(slots):
            a_copies.append(pltpu.make_async_copy(
                ints_ref.at[0, g, k], a_buf.at[pl.ds((g * slots + k) * bs, bs), :], a_sem.at[g * slots + k]))
    for copy in a_copies:
        copy.start()

    barrier = pltpu.get_barrier_semaphore()
    for off in offs:
        pl.semaphore_signal(barrier, inc=1, device_id={"pair": lax.rem(q + off, pairs), "blk": b}, device_id_type=MESH)
    for j in range(1, chips):
        pl.semaphore_signal(barrier, inc=1, device_id={"pair": q, "blk": lax.rem(b + 2 * j, blks)}, device_id_type=MESH)
    pl.semaphore_signal(barrier, inc=1, device_id={"pair": q, "blk": sib}, device_id_type=MESH)

    t_id = lax.broadcasted_iota(jnp.int32, (half, bs), 0)
    i_id = lax.broadcasted_iota(jnp.int32, (half, bs), 1)
    pick = jnp.where(i_id == 2 * t_id + core, 1.0, 0.0).astype(BF16)
    mine = jnp.dot(pick, metric_ref[...], preferred_element_type=F32).astype(BF16)
    met_all[core, pl.ds(pl.multiple_of(q * half, half), half), :] = mine
    dens_all[b] = jnp.zeros(dens_all.shape[1:], BF16)
    dens_all[b, 0:sig, :] = dens_ref[...]

    pl.semaphore_wait(barrier, len(offs) + chips)

    d_out = []
    for j in range(chips):
        to = sib if j == 0 else lax.rem(b + 2 * j, blks)
        copy = pltpu.make_async_remote_copy(
            src_ref=dens_all.at[b], dst_ref=dens_all.at[b], send_sem=dsend.at[j], recv_sem=drecv.at[j],
            device_id={"pair": q, "blk": to}, device_id_type=MESH)
        copy.start()
        d_out.append(copy)
    m_out = []
    for n, off in enumerate(offs):
        part = met_all.at[core, pl.ds(pl.multiple_of(q * half, half), half), :]
        copy = pltpu.make_async_remote_copy(
            src_ref=part, dst_ref=part, send_sem=msend.at[n], recv_sem=mrecv.at[n],
            device_id={"pair": lax.rem(q + off, pairs), "blk": b}, device_id_type=MESH)
        copy.start()
        m_out.append(copy)

    lag = lax.broadcasted_iota(jnp.int32, (bs, cols), 1) - sig * lax.broadcasted_iota(jnp.int32, (bs, cols), 0)
    for s in range(sig):
        perm[s * bs:(s + 1) * bs, :] = jnp.where(lag == s, 1.0, 0.0).astype(BF16)

    for j in range(1, chips):
        src = lax.rem(b + blks - 2 * j, blks)
        pltpu.make_async_remote_copy(
            src_ref=dens_all.at[src], dst_ref=dens_all.at[src], send_sem=dsend.at[j], recv_sem=drecv.at[j],
            device_id={"pair": q, "blk": sib}, device_id_type=MESH).wait_recv()
        copy = pltpu.make_async_remote_copy(
            src_ref=dens_all.at[src], dst_ref=dens_all.at[src], send_sem=dsend.at[chips + j - 1],
            recv_sem=drecv.at[chips + j - 1], device_id={"pair": q, "blk": sib}, device_id_type=MESH)
        copy.start()
        d_out.append(copy)
    for j in range(chips):
        src = lax.rem(sib + blks - 2 * j, blks)
        pltpu.make_async_remote_copy(
            src_ref=dens_all.at[src], dst_ref=dens_all.at[src], send_sem=dsend.at[0],
            recv_sem=drecv.at[0 if j == 0 else chips + j - 1],
            device_id={"pair": q, "blk": sib}, device_id_type=MESH).wait_recv()

    lane = lax.broadcasted_iota(jnp.int32, (16, 128), 1)
    p_id = lax.broadcasted_iota(jnp.int32, (pn, 128), 0)
    p_lane = lax.broadcasted_iota(jnp.int32, (pn, 128), 1)
    for g in range(blks):
        filled = jnp.full((pn, 128), cnt_ref[0, g], jnp.int32)
        for k in range(0, slots, 2):
            nus = [jnp.full((16, 128), nu_ref[0, g, k + e], jnp.int32) for e in range(2)]
            found = [jnp.zeros((16, 128), F32), jnp.zeros((16, 128), F32)]
            for t in range(dens_ref.shape[1] // 128):
                tile = dens_all[g, :, t * 128:(t + 1) * 128].astype(F32)
                for e in range(2):
                    found[e] = jnp.where((nus[e] >> 1) == t, tile, found[e])
            tiles, marks = [], []
            for e in range(2):
                turned = pltpu.roll(found[e], 64, 1)
                tiles.append(jnp.where((nus[e] & 1) != e, turned, found[e]))
                target = jnp.full((pn, 128), p_ref[0, g, k + e], jnp.int32)
                marks.append(jnp.where(filled > k + e, target, -1))
            both = jnp.where(lane < 64, tiles[0], tiles[1])
            mask = jnp.where(p_lane < 64, marks[0], marks[1]) == p_id
            c0 = (g * slots + k) * bs
            for s in range(sig):
                row = jnp.broadcast_to(both[s:s + 1, :], (pn, 128))
                lbuf[s * pn:(s + 1) * pn, c0:c0 + 128] = jnp.where(mask, row, 0.0)

    for copy in a_copies:
        copy.wait()
    left = lbuf[...].astype(BF16)
    width = 512
    tiles_per = width // 128

    @pl.loop(0, bs * bs // width)
    def _(j):
        r = jnp.dot(left, a_buf[:, pl.ds(pl.multiple_of(j * width, width), width)], preferred_element_type=F32)
        for s in range(sig):
            for t in range(tiles_per):
                row0 = pl.multiple_of((s * half + j * tiles_per + t) * pn, 8)
                zbuf[pl.ds(row0, pn), :] = r[s * pn:(s + 1) * pn, t * 128:(t + 1) * 128]

    for n, off in enumerate(offs):
        src = lax.rem(q + pairs - off, pairs)
        part = met_all.at[core, pl.ds(pl.multiple_of(src * half, half), half), :]
        pltpu.make_async_remote_copy(
            src_ref=part, dst_ref=part, send_sem=msend.at[n], recv_sem=mrecv.at[n],
            device_id={"pair": q, "blk": sib}, device_id_type=MESH).wait_recv()
    last = len(offs)
    m_fwd = pltpu.make_async_remote_copy(
        src_ref=met_all.at[core], dst_ref=met_all.at[core], send_sem=msend.at[last], recv_sem=mrecv.at[last],
        device_id={"pair": q, "blk": sib}, device_id_type=MESH)
    m_fwd.start()
    m_out.append(m_fwd)

    low = lax.broadcasted_iota(jnp.int32, (half, 128), 1) < 64

    @pl.loop(0, pn)
    def _(p):
        for s in range(0, sig, 2):
            z0 = zbuf[pl.ds(s * half * pn + p, half, stride=pn), :]
            z1 = zbuf[pl.ds((s + 1) * half * pn + p, half, stride=pn), :]
            x0 = jnp.where(low, z0, pltpu.roll(z1, 64, 1))
            x1 = jnp.where(low, pltpu.roll(z0, 64, 1), z1)
            at = pl.ds(pl.multiple_of(p * half, half), half)
            xbuf[0, at, s * bs:s * bs + 128] = x0.astype(BF16)
            xbuf[1, at, s * bs:s * bs + 128] = x1.astype(BF16)

    pltpu.make_async_remote_copy(
        src_ref=met_all.at[1 - core], dst_ref=met_all.at[1 - core], send_sem=msend.at[last], recv_sem=mrecv.at[last],
        device_id={"pair": q, "blk": sib}, device_id_type=MESH).wait_recv()

    block = 256
    parts = cols // block
    y_out = []
    for c in range(parts):
        span = slice(c * block, (c + 1) * block)
        total = None
        for h in range(2):
            xp = jnp.dot(xbuf[h], perm[:, span], preferred_element_type=F32).astype(BF16)
            term = lax.dot_general(met_all[h], xp, (((0,), (0,)), ((), ())), preferred_element_type=F32)
            total = term if total is None else total + term
        ysend[c] = total.astype(BF16).reshape(pairs, bs, block)
        for n, off in enumerate(offs):
            to = lax.rem(q + off, pairs)
            copy = pltpu.make_async_remote_copy(
                src_ref=ysend.at[c, to], dst_ref=out_ref.at[q, 0, :, span], send_sem=ysems.at[c, n],
                recv_sem=yrecv.at[c, n], device_id={"pair": to, "blk": b}, device_id_type=MESH)
            copy.start()
            y_out.append(copy)
        copy = pltpu.make_async_copy(ysend.at[c, q], out_ref.at[q, 0, :, span], own_sem.at[c])
        copy.start()

    for c in range(parts):
        span = slice(c * block, (c + 1) * block)
        for n, off in enumerate(offs):
            src = lax.rem(q + pairs - off, pairs)
            pltpu.make_async_remote_copy(
                src_ref=ysend.at[c, src], dst_ref=out_ref.at[src, 0, :, span], send_sem=ysems.at[c, n],
                recv_sem=yrecv.at[c, n], device_id={"pair": src, "blk": b}, device_id_type=MESH).wait_recv()
        pltpu.make_async_copy(ysend.at[c, q], out_ref.at[q, 0, :, span], own_sem.at[c]).wait()
    for copy in d_out + m_out + y_out:
        copy.wait_send()


def solution(mesh):
    pairs, blks = mesh.shape["pair"], mesh.shape["blk"]

    def per_device(integrals, density, metric, nu_local, p_index, counts):
        _, groups, slots, bs, wide = integrals.shape
        sig, panel = density.shape
        aux = metric.shape[1]
        cols = sig * bs
        pn = aux // bs
        half = bs // 2
        n_off = pairs - 1
        chips = blks // 2
        block = 256
        parts = cols // block
        vmem = pl.BlockSpec(memory_space=pltpu.VMEM)
        smem = pl.BlockSpec(memory_space=pltpu.SMEM)
        anyw = pl.BlockSpec(memory_space=pl.ANY)
        dma = pltpu.SemaphoreType.DMA
        return pl.pallas_call(
            functools.partial(kernel, pairs, blks),
            out_shape=jax.ShapeDtypeStruct((pairs, 1, bs, cols), BF16),
            in_specs=[smem, smem, smem, anyw, vmem, vmem],
            out_specs=anyw,
            scratch_shapes=[
                pltpu.VMEM((groups * slots * bs, wide), BF16),
                pltpu.VMEM((blks, 16, panel), BF16),
                pltpu.VMEM((2, pn * half, aux), BF16),
                pltpu.VMEM((sig * half * pn, 128), F32),
                pltpu.VMEM((2, pn * half, cols), BF16),
                pltpu.VMEM((cols, cols), BF16),
                pltpu.VMEM((parts, pairs, bs, block), BF16),
                pltpu.VMEM((sig * pn, groups * slots * bs), F32),
                dma((groups * slots,)),
                dma((2 * chips,)),
                dma((2 * chips,)),
                dma((n_off + 1,)),
                dma((n_off + 1,)),
                dma((parts, n_off)),
                dma((parts, n_off)),
                dma((parts,)),
            ],
            compiler_params=pltpu.CompilerParams(
                collective_id=0, has_side_effects=True, vmem_limit_bytes=56 * 1024 * 1024
            ),
            cost_estimate=pl.CostEstimate(flops=2000000000, bytes_accessed=6000000, transcendentals=0),
        )(nu_local, p_index, counts, integrals, density, metric)

    in_specs = (
        P(("pair", "blk"), None, None, None, None),
        P(None, "blk"),
        P("pair", None),
        P(("pair", "blk"), None, None),
        P(("pair", "blk"), None, None),
        P(("pair", "blk"), None),
    )
    return jax.shard_map(
        per_device, mesh=mesh, in_specs=in_specs, out_specs=P(None, "blk", "pair", None), check_vma=False
    )
```

time: 125 us -> 40.3 us (0.32)
  blocking collectives: 57.6 us -> 0 us
  Pallas kernels: 0 us -> 35.3 us
  local copies, waits for them, and re-layouts: 32.6 us -> 4.75 us
  matrix products: 18.4 us -> 0 us
  waiting for transfers between devices: 7.86 us -> 0 us
  other arithmetic: 6.87 us -> 0 us
    pallas_call x0 -> x1, Pallas kernels: none -> 35.3 us  [per_device(): pl.pallas_call(functools.partial(kernel, pairs, blks), out_shape=jax.Shap...]
    all_gather x1 -> x0, blocking collectives: 32.7 us -> none  [per_device(): whole_metric = lax.all_gather(metric, 'pair', axis=0, tiled=True)]
    all_to_all x1 -> x0, blocking collectives: 24.9 us -> none  [per_device(): lax.all_to_all(result_rows, 'pair', split_axis=2, concat_axis=0, tiled=True)]
    reshape x5 -> x0, local copies, waits for them, and re-layouts: 21.3 us -> none  [the longest x4 19.7 us: per_device(): contrib = contrib.reshape(slot_count, block_width, block_width * columns)]
    dot_general x6 -> x0, matrix products: 18.4 us -> none  [the longest x4 16.4 us: per_device(): jnp.einsum('sgn,gnx->gxs', dens_cols, cube, preferred_element_type=jnp.fl...]
    ppermute x3 -> x0, waiting for transfers between devices: 7.86 us -> none  [passed_along(): return lax.ppermute(block, axis, route)]
    unnamed x1 -> x0, other arithmetic: 5.43 us -> none
    gather x8 -> x0, local copies, waits for them, and re-layouts: 3.23 us -> none  [per_device(): dens_cols = jnp.take(panel_now, col_index, axis=1)]
  transfers between devices with their start and end apart: 3 -> 0, of which waited for: 2 -> 0; matrix products, arithmetic and copies ran while one was open for 12% -> 0% of each run, Pallas kernels for 0% -> 0%
where the time goes in v1:
time: 40.3 us; the launch traced here: 40.1 us
  Pallas kernels  35.3 us (88%)
  local copies, waits for them, and re-layouts  4.75 us (12%)
    pallas_call x1, Pallas kernels, per_device(): pl.pallas_call(functools.partial(kernel, pairs, blks), out_shape=jax.Shap...  35.3 us
    unnamed x3, local copies, waits for them, and re-layouts  4.75 us

profile of v1, /device:TPU:0, one launch (start us, length us, event | category | flops | bytes accessed | tf_op | source)
XLA Modules:
  0.0 40.1 jit_solution(17697195509158056749)
XLA Ops:
  0.0 1.3 %copy.7.nu_ref = s32[1,4,2]{2,1,0:T(4,128)} copy(s32[1,4,2]{1,2,0:T(2,128)} %param.9) | data formatting | bytes 64 | tf_op args[3]
  1.3 1.3 %copy.8.p_ref = s32[1,4,2]{2,1,0:T(4,128)} copy(s32[1,4,2]{1,2,0:T(2,128)} %param.10) | data formatting | bytes 64 | tf_op args[4]
  2.7 35.3 %shard_map.64 = bf16[8,1,64,768]{3,2,1,0:T(8,128)(2,1)} custom-call(s32[1,4,2]{2,1,0:T(4,128)} %copy.7.nu_ref, s32[1,4,2]{2,1,0:T(4,128)} %copy.8.p_ref, s32[1,4]{1,0:T(1,128)} %cnt_ref.1, bf16[1,4,2,64,4096]{4,3,2,1,0:T(8,128)(2,1)} %ints_ref.1, bf16[12,4096]{1,0:T(8,128)(2,1)} %dens_ref.1, bf16[64,512]{1,0:T(8,128)(2,1)} %metric_ref.1), custom_call_target="tpu_custom_call" | custom-call | flops 2000000000 | bytes 6000000 | tf_op jit(solution)/shard_map/pallas_call | solution.py:220
  38.0 2.1 %copy.10 = bf16[8,1,64,768]{3,2,1,0:T(8,128)(2,1)} copy(bf16[8,1,64,768]{3,2,1,0:T(8,128)(2,1)} %shard_map.64) | data formatting | bytes 1572864

commit v2 on v1

v2 whole, which is shorter than its diff:
```python
import functools

import jax
import jax.numpy as jnp
from jax import lax
from jax.experimental import pallas as pl
from jax.experimental.pallas import tpu as pltpu
from jax.sharding import PartitionSpec as P

MESH = pl.DeviceIdType.MESH
BF16 = jnp.bfloat16
F32 = jnp.float32


def offsets_far_first(count):
    return sorted(range(1, count), key=lambda off: -min(off, count - off))


def kernel(pairs, blks, nu_ref, p_ref, cnt_ref, ints_ref, dens_ref, metric_ref, out_ref,
           a_buf, dens_pad, req_out, req_in, rep_out, rep_in, met_all, met_t, zbuf, xbuf, perm, ysend, lbuf,
           a_sem, req_s, req_r, rep_s, rep_r, msend, mrecv, fsend, frecv, ysems, yrecv, own_sem):
    q = lax.axis_index("pair")
    b = lax.axis_index("blk")
    core = lax.rem(b, 2)
    sib = b + 1 - 2 * core
    slots = p_ref.shape[1]
    bs = metric_ref.shape[0]
    half = bs // 2
    aux = metric_ref.shape[1]
    sig = dens_ref.shape[0]
    cols = sig * bs
    pn = aux // bs
    offs = offsets_far_first(pairs)

    a_copies = []
    for g in range(blks):
        for k in range(slots):
            a_copies.append(pltpu.make_async_copy(
                ints_ref.at[0, g, k], a_buf.at[pl.ds((g * slots + k) * bs, bs), :], a_sem.at[g * slots + k]))
    for copy in a_copies:
        copy.start()

    barrier = pltpu.get_barrier_semaphore()
    for off in offs:
        pl.semaphore_signal(barrier, inc=1, device_id={"pair": lax.rem(q + off, pairs), "blk": b}, device_id_type=MESH)
    for j in range(1, blks):
        pl.semaphore_signal(barrier, inc=1, device_id={"pair": q, "blk": lax.rem(b + j, blks)}, device_id_type=MESH)

    row_id = lax.broadcasted_iota(jnp.int32, (8, 128), 0)
    for j in range(1, blks):
        g = lax.rem(b + j, blks)
        tile = jnp.full((8, 128), nu_ref[0, 0, g], jnp.int32)
        for k in range(1, slots):
            tile = jnp.where(row_id == k, nu_ref[0, k, g], tile)
        req_out[j] = tile

    t_id = lax.broadcasted_iota(jnp.int32, (half, bs), 0)
    i_id = lax.broadcasted_iota(jnp.int32, (half, bs), 1)
    pick = jnp.where(i_id == 2 * t_id + core, 1.0, 0.0).astype(BF16)
    mine = jnp.dot(pick, metric_ref[...], preferred_element_type=F32).astype(BF16)
    met_all[core, pl.ds(pl.multiple_of(q * half, half), half), :] = mine
    dens_pad[...] = jnp.zeros(dens_pad.shape, BF16)
    dens_pad[0:sig, :] = dens_ref[...]

    pl.semaphore_wait(barrier, len(offs) + blks - 1)

    def blk_copy(src, dst, send, recv, j, to):
        return pltpu.make_async_remote_copy(
            src_ref=src.at[j], dst_ref=dst.at[j], send_sem=send.at[j], recv_sem=recv.at[j],
            device_id={"pair": q, "blk": to}, device_id_type=MESH)

    sent = []
    for j in range(1, blks):
        copy = blk_copy(req_out, req_in, req_s, req_r, j, lax.rem(b + j, blks))
        copy.start()
        sent.append(copy)
    m_out = []
    for n, off in enumerate(offs):
        part = met_all.at[core, pl.ds(pl.multiple_of(q * half, half), half), :]
        copy = pltpu.make_async_remote_copy(
            src_ref=part, dst_ref=part, send_sem=msend.at[n], recv_sem=mrecv.at[n],
            device_id={"pair": lax.rem(q + off, pairs), "blk": b}, device_id_type=MESH)
        copy.start()
        m_out.append(copy)

    def to_sibling(half_id, src, n):
        part = met_all.at[half_id, pl.ds(pl.multiple_of(src * half, half), half), :]
        return pltpu.make_async_remote_copy(
            src_ref=part, dst_ref=part, send_sem=fsend.at[n], recv_sem=frecv.at[n],
            device_id={"pair": q, "blk": sib}, device_id_type=MESH)

    copy = to_sibling(core, q, len(offs))
    copy.start()
    m_out.append(copy)

    lane = lax.broadcasted_iota(jnp.int32, (16, 128), 1)

    def columns_of(indices):
        found = [[jnp.zeros((16, 128), F32) for _ in range(slots)] for _ in indices]
        for t in range(dens_ref.shape[1] // 128):
            tile = dens_pad[:, t * 128:(t + 1) * 128].astype(F32)
            for a, nus in enumerate(indices):
                for k in range(slots):
                    found[a][k] = jnp.where((nus[k] >> 1) == t, tile, found[a][k])
        out = []
        for a, nus in enumerate(indices):
            sides = []
            for k in range(slots):
                turned = pltpu.roll(found[a][k], 64, 1)
                sides.append(jnp.where((nus[k] & 1) != k, turned, found[a][k]))
            out.append(jnp.where(lane < 64, sides[0], sides[1]))
        return out

    p_id = lax.broadcasted_iota(jnp.int32, (pn, 128), 0)
    p_lane = lax.broadcasted_iota(jnp.int32, (pn, 128), 1)

    def put(g, both):
        filled = jnp.full((pn, 128), cnt_ref[0, g], jnp.int32)
        marks = [jnp.where(filled > k, jnp.full((pn, 128), p_ref[0, k, g], jnp.int32), -1) for k in range(slots)]
        mask = jnp.where(p_lane < 64, marks[0], marks[1]) == p_id
        at = pl.ds(pl.multiple_of(g * 128, 128), 128)
        for s in range(sig):
            row = jnp.broadcast_to(both[s:s + 1, :], (pn, 128))
            lbuf[s * pn:(s + 1) * pn, at] = jnp.where(mask, row, 0.0)

    own = columns_of([[jnp.full((16, 128), nu_ref[0, k, b], jnp.int32) for k in range(slots)]])
    put(b, own[0])
    for j in range(1, blks):
        blk_copy(req_out, req_in, req_s, req_r, j, lax.rem(b + j, blks)).wait_recv()
    asked = [[jnp.broadcast_to(req_in[j, k:k + 1, :], (16, 128)) for k in range(slots)] for j in range(1, blks)]
    for first in range(0, blks - 1, 4):
        for n, both in enumerate(columns_of(asked[first:first + 4])):
            j = first + n + 1
            rep_out[j] = both.astype(BF16)
            copy = blk_copy(rep_out, rep_in, rep_s, rep_r, j, lax.rem(b + blks - j, blks))
            copy.start()
            sent.append(copy)

    lag = lax.broadcasted_iota(jnp.int32, (bs, cols), 1) - sig * lax.broadcasted_iota(jnp.int32, (bs, cols), 0)
    for s in range(sig):
        perm[s * bs:(s + 1) * bs, :] = jnp.where(lag == s, 1.0, 0.0).astype(BF16)

    for j in range(1, blks):
        blk_copy(rep_out, rep_in, rep_s, rep_r, j, lax.rem(b + j, blks)).wait_recv()
        put(lax.rem(b + j, blks), rep_in[j].astype(F32))

    for copy in a_copies:
        copy.wait()
    left = lbuf[...].astype(BF16)
    width = 512
    tiles_per = width // 128

    @pl.loop(0, bs * bs // width)
    def _(j):
        r = jnp.dot(left, a_buf[:, pl.ds(pl.multiple_of(j * width, width), width)], preferred_element_type=F32)
        for s in range(sig):
            for t in range(tiles_per):
                row0 = pl.multiple_of((s * half + j * tiles_per + t) * pn, 8)
                zbuf[pl.ds(row0, pn), :] = r[s * pn:(s + 1) * pn, t * 128:(t + 1) * 128]

    for n, off in enumerate(offs):
        src = lax.rem(q + pairs - off, pairs)
        part = met_all.at[core, pl.ds(pl.multiple_of(src * half, half), half), :]
        pltpu.make_async_remote_copy(
            src_ref=part, dst_ref=part, send_sem=msend.at[n], recv_sem=mrecv.at[n],
            device_id={"pair": q, "blk": sib}, device_id_type=MESH).wait_recv()
        copy = to_sibling(core, src, n)
        copy.start()
        m_out.append(copy)

    low = lax.broadcasted_iota(jnp.int32, (half, 128), 1) < 64

    @pl.loop(0, pn)
    def _(p):
        for s in range(0, sig, 2):
            z0 = zbuf[pl.ds(s * half * pn + p, half, stride=pn), :]
            z1 = zbuf[pl.ds((s + 1) * half * pn + p, half, stride=pn), :]
            x0 = jnp.where(low, z0, pltpu.roll(z1, 64, 1))
            x1 = jnp.where(low, pltpu.roll(z0, 64, 1), z1)
            at = pl.ds(pl.multiple_of(p * half, half), half)
            xbuf[0, at, s * bs:s * bs + 128] = x0.astype(BF16)
            xbuf[1, at, s * bs:s * bs + 128] = x1.astype(BF16)

    met_t[core] = met_all[core].T
    for n, off in enumerate(offs + [0]):
        to_sibling(1 - core, lax.rem(q + pairs - off, pairs), n).wait_recv()
    met_t[1 - core] = met_all[1 - core].T

    block = 256
    parts = cols // block
    y_out = []
    for c in range(parts):
        span = slice(c * block, (c + 1) * block)
        total = None
        for h in range(2):
            xp = jnp.dot(xbuf[h], perm[:, span], preferred_element_type=F32).astype(BF16)
            term = jnp.dot(met_t[h], xp, preferred_element_type=F32)
            total = term if total is None else total + term
        ysend[c] = total.astype(BF16).reshape(pairs, bs, block)
        for n, off in enumerate(offs):
            to = lax.rem(q + off, pairs)
            copy = pltpu.make_async_remote_copy(
                src_ref=ysend.at[c, to], dst_ref=out_ref.at[q, 0, :, span], send_sem=ysems.at[c, n],
                recv_sem=yrecv.at[c, n], device_id={"pair": to, "blk": b}, device_id_type=MESH)
            copy.start()
            y_out.append(copy)
        copy = pltpu.make_async_copy(ysend.at[c, q], out_ref.at[q, 0, :, span], own_sem.at[c])
        copy.start()

    for c in range(parts):
        span = slice(c * block, (c + 1) * block)
        for n, off in enumerate(offs):
            src = lax.rem(q + pairs - off, pairs)
            pltpu.make_async_remote_copy(
                src_ref=ysend.at[c, src], dst_ref=out_ref.at[src, 0, :, span], send_sem=ysems.at[c, n],
                recv_sem=yrecv.at[c, n], device_id={"pair": src, "blk": b}, device_id_type=MESH).wait_recv()
        pltpu.make_async_copy(ysend.at[c, q], out_ref.at[q, 0, :, span], own_sem.at[c]).wait()
    for copy in sent + m_out + y_out:
        copy.wait_send()


def solution(mesh):
    pairs, blks = mesh.shape["pair"], mesh.shape["blk"]

    def per_device(integrals, density, metric, nu_local, p_index, counts):
        _, groups, slots, bs, wide = integrals.shape
        sig, panel = density.shape
        aux = metric.shape[1]
        cols = sig * bs
        pn = aux // bs
        half = bs // 2
        n_off = pairs - 1
        block = 256
        parts = cols // block
        vmem = pl.BlockSpec(memory_space=pltpu.VMEM)
        smem = pl.BlockSpec(memory_space=pltpu.SMEM)
        anyw = pl.BlockSpec(memory_space=pl.ANY)
        dma = pltpu.SemaphoreType.DMA
        return pl.pallas_call(
            functools.partial(kernel, pairs, blks),
            out_shape=pltpu.VMEM((pairs, 1, bs, cols), BF16),
            in_specs=[smem, smem, smem, anyw, vmem, vmem],
            out_specs=vmem,
            scratch_shapes=[
                pltpu.VMEM((groups * slots * bs, wide), BF16),
                pltpu.VMEM((16, panel), BF16),
                pltpu.VMEM((blks, 8, 128), jnp.int32),
                pltpu.VMEM((blks, 8, 128), jnp.int32),
                pltpu.VMEM((blks, 16, 128), BF16),
                pltpu.VMEM((blks, 16, 128), BF16),
                pltpu.VMEM((2, pn * half, aux), BF16),
                pltpu.VMEM((2, aux, pn * half), BF16),
                pltpu.VMEM((sig * half * pn, 128), F32),
                pltpu.VMEM((2, pn * half, cols), BF16),
                pltpu.VMEM((cols, cols), BF16),
                pltpu.VMEM((parts, pairs, bs, block), BF16),
                pltpu.VMEM((sig * pn, groups * slots * bs), F32),
                dma((groups * slots,)),
                dma((blks,)),
                dma((blks,)),
                dma((blks,)),
                dma((blks,)),
                dma((n_off,)),
                dma((n_off,)),
                dma((n_off + 1,)),
                dma((n_off + 1,)),
                dma((parts, n_off)),
                dma((parts, n_off)),
                dma((parts,)),
            ],
            compiler_params=pltpu.CompilerParams(
                collective_id=0, has_side_effects=True, vmem_limit_bytes=56 * 1024 * 1024
            ),
            cost_estimate=pl.CostEstimate(flops=2000000000, bytes_accessed=6000000, transcendentals=0),
        )(jnp.swapaxes(nu_local, 1, 2), jnp.swapaxes(p_index, 1, 2), counts, integrals, density, metric)

    in_specs = (
        P(("pair", "blk"), None, None, None, None),
        P(None, "blk"),
        P("pair", None),
        P(("pair", "blk"), None, None),
        P(("pair", "blk"), None, None),
        P(("pair", "blk"), None),
    )
    return jax.shard_map(
        per_device, mesh=mesh, in_specs=in_specs, out_specs=P(None, "blk", "pair", None), check_vma=False
    )
```

time: 40.3 us -> 35.7 us (0.89)
  local copies, waits for them, and re-layouts: 4.75 us -> 0.88 us
  Pallas kernels: 35.3 us -> 34.6 us
    unnamed x3 -> x1, local copies, waits for them, and re-layouts: 4.75 us -> 0.88 us
    pallas_call x1, Pallas kernels: 35.3 us -> 34.6 us  [per_device(): pl.pallas_call(functools.partial(kernel, pairs, blks), out_shape=pltpu.VM...]
where the time goes in v2:
time: 35.7 us; the launch traced here: 35.5 us
  Pallas kernels  34.6 us (97%)
  local copies, waits for them, and re-layouts  0.88 us (2%)
    pallas_call x1, Pallas kernels, per_device(): pl.pallas_call(functools.partial(kernel, pairs, blks), out_shape=pltpu.VM...  34.6 us
    unnamed x1, local copies, waits for them, and re-layouts  0.88 us

profile of v2, /device:TPU:0, one launch (start us, length us, event | category | flops | bytes accessed | tf_op | source)
XLA Modules:
  0.0 35.5 jit_solution(17680733781221532401)
XLA Ops:
  0.0 34.6 %shard_map.64 = bf16[8,1,64,768]{3,2,1,0:T(8,128)(2,1)S(1)} custom-call(s32[1,2,4]{2,1,0:T(2,128)} %bitcast.2, s32[1,2,4]{2,1,0:T(2,128)} %bitcast.3, s32[1,4]{1,0:T(1,128)} %cnt_ref.1, bf16[1,4,2,64,4096]{4,3,2,1,0:T(8,128)(2,1)} %ints_ref.1, bf16[12,4096]{1,0:T(8,128)(2,1)} %dens_ref.1, bf16[64,512]{1,0:T(8,128)(2,1)} %metric_ref.1), custom_call_target="tpu_custom_call" | custom-call | flops 2000000000 | bytes 6000000 | tf_op jit(solution)/shard_map/pallas_call | solution.py:239
  34.6 0.9 %copy.8 = bf16[8,1,64,768]{3,2,1,0:T(8,128)(2,1)} copy(bf16[8,1,64,768]{3,2,1,0:T(8,128)(2,1)S(1)} %shard_map.64) | data formatting | bytes 1572864

commit v3 on v2

--- a/solution.py
+++ b/solution.py
@@ -17,8 +17,8 @@
 
 
 def kernel(pairs, blks, nu_ref, p_ref, cnt_ref, ints_ref, dens_ref, metric_ref, out_ref,
-           a_buf, dens_pad, req_out, req_in, rep_out, rep_in, met_all, met_t, zbuf, xbuf, perm, ysend, lbuf,
-           a_sem, req_s, req_r, rep_s, rep_r, msend, mrecv, fsend, frecv, ysems, yrecv, own_sem):
+           a_buf, dens_in, met_in, req_out, req_in, rep_out, rep_in, met_all, met_t, order, xbuf, perm, ysend, lbuf,
+           a_sem, in_sem, req_s, req_r, rep_s, rep_r, msend, mrecv, fsend, frecv, ysems, yrecv, own_sem):
     q = lax.axis_index("pair")
     b = lax.axis_index("blk")
     core = lax.rem(b, 2)
@@ -37,14 +37,19 @@
         for k in range(slots):
             a_copies.append(pltpu.make_async_copy(
                 ints_ref.at[0, g, k], a_buf.at[pl.ds((g * slots + k) * bs, bs), :], a_sem.at[g * slots + k]))
-    for copy in a_copies:
-        copy.start()
 
     barrier = pltpu.get_barrier_semaphore()
     for off in offs:
         pl.semaphore_signal(barrier, inc=1, device_id={"pair": lax.rem(q + off, pairs), "blk": b}, device_id_type=MESH)
     for j in range(1, blks):
         pl.semaphore_signal(barrier, inc=1, device_id={"pair": q, "blk": lax.rem(b + j, blks)}, device_id_type=MESH)
+
+    dens_load = pltpu.make_async_copy(dens_ref, dens_in, in_sem.at[0])
+    met_load = pltpu.make_async_copy(metric_ref, met_in, in_sem.at[1])
+    met_load.start()
+    dens_load.start()
+    for copy in a_copies:
+        copy.start()
 
     row_id = lax.broadcasted_iota(jnp.int32, (8, 128), 0)
     for j in range(1, blks):
@@ -54,14 +59,6 @@
             tile = jnp.where(row_id == k, nu_ref[0, k, g], tile)
         req_out[j] = tile
 
-    t_id = lax.broadcasted_iota(jnp.int32, (half, bs), 0)
-    i_id = lax.broadcasted_iota(jnp.int32, (half, bs), 1)
-    pick = jnp.where(i_id == 2 * t_id + core, 1.0, 0.0).astype(BF16)
-    mine = jnp.dot(pick, metric_ref[...], preferred_element_type=F32).astype(BF16)
-    met_all[core, pl.ds(pl.multiple_of(q * half, half), half), :] = mine
-    dens_pad[...] = jnp.zeros(dens_pad.shape, BF16)
-    dens_pad[0:sig, :] = dens_ref[...]
-
     pl.semaphore_wait(barrier, len(offs) + blks - 1)
 
     def blk_copy(src, dst, send, recv, j, to):
@@ -69,11 +66,18 @@
             src_ref=src.at[j], dst_ref=dst.at[j], send_sem=send.at[j], recv_sem=recv.at[j],
             device_id={"pair": q, "blk": to}, device_id_type=MESH)
 
+    rep_out[...] = jnp.zeros(rep_out.shape, BF16)
     sent = []
     for j in range(1, blks):
         copy = blk_copy(req_out, req_in, req_s, req_r, j, lax.rem(b + j, blks))
         copy.start()
         sent.append(copy)
+    t_id = lax.broadcasted_iota(jnp.int32, (half, bs), 0)
+    i_id = lax.broadcasted_iota(jnp.int32, (half, bs), 1)
+    pick = jnp.where(i_id == 2 * t_id + core, 1.0, 0.0).astype(BF16)
+    met_load.wait()
+    mine = jnp.dot(pick, met_in[...], preferred_element_type=F32).astype(BF16)
+    met_all[core, pl.ds(pl.multiple_of(q * half, half), half), :] = mine
     m_out = []
     for n, off in enumerate(offs):
         part = met_all.at[core, pl.ds(pl.multiple_of(q * half, half), half), :]
@@ -89,16 +93,14 @@
             src_ref=part, dst_ref=part, send_sem=fsend.at[n], recv_sem=frecv.at[n],
             device_id={"pair": q, "blk": sib}, device_id_type=MESH)
 
-    copy = to_sibling(core, q, len(offs))
-    copy.start()
-    m_out.append(copy)
-
-    lane = lax.broadcasted_iota(jnp.int32, (16, 128), 1)
+
+    lane = lax.broadcasted_iota(jnp.int32, (sig, 128), 1)
+    dens_load.wait()
 
     def columns_of(indices):
-        found = [[jnp.zeros((16, 128), F32) for _ in range(slots)] for _ in indices]
+        found = [[jnp.zeros((sig, 128), F32) for _ in range(slots)] for _ in indices]
         for t in range(dens_ref.shape[1] // 128):
-            tile = dens_pad[:, t * 128:(t + 1) * 128].astype(F32)
+            tile = dens_in[:, t * 128:(t + 1) * 128].astype(F32)
             for a, nus in enumerate(indices):
                 for k in range(slots):
                     found[a][k] = jnp.where((nus[k] >> 1) == t, tile, found[a][k])
@@ -123,15 +125,15 @@
             row = jnp.broadcast_to(both[s:s + 1, :], (pn, 128))
             lbuf[s * pn:(s + 1) * pn, at] = jnp.where(mask, row, 0.0)
 
-    own = columns_of([[jnp.full((16, 128), nu_ref[0, k, b], jnp.int32) for k in range(slots)]])
+    own = columns_of([[jnp.full((sig, 128), nu_ref[0, k, b], jnp.int32) for k in range(slots)]])
     put(b, own[0])
     for j in range(1, blks):
         blk_copy(req_out, req_in, req_s, req_r, j, lax.rem(b + j, blks)).wait_recv()
-    asked = [[jnp.broadcast_to(req_in[j, k:k + 1, :], (16, 128)) for k in range(slots)] for j in range(1, blks)]
+    asked = [[jnp.broadcast_to(req_in[j, k:k + 1, :], (sig, 128)) for k in range(slots)] for j in range(1, blks)]
     for first in range(0, blks - 1, 4):
         for n, both in enumerate(columns_of(asked[first:first + 4])):
             j = first + n + 1
-            rep_out[j] = both.astype(BF16)
+            rep_out[j, 0:sig, :] = both.astype(BF16)
             copy = blk_copy(rep_out, rep_in, rep_s, rep_r, j, lax.rem(b + blks - j, blks))
             copy.start()
             sent.append(copy)
@@ -139,6 +141,11 @@
     lag = lax.broadcasted_iota(jnp.int32, (bs, cols), 1) - sig * lax.broadcasted_iota(jnp.int32, (bs, cols), 0)
     for s in range(sig):
         perm[s * bs:(s + 1) * bs, :] = jnp.where(lag == s, 1.0, 0.0).astype(BF16)
+
+    shift = pn.bit_length() - 1
+    r_id = lax.broadcasted_iota(jnp.int32, order.shape, 0)
+    c_id = lax.broadcasted_iota(jnp.int32, order.shape, 1)
+    order[...] = jnp.where(c_id == (r_id & (pn - 1)) * half + (r_id >> shift), 1.0, 0.0).astype(BF16)
 
     for j in range(1, blks):
         blk_copy(rep_out, rep_in, rep_s, rep_r, j, lax.rem(b + j, blks)).wait_recv()
@@ -149,14 +156,19 @@
     left = lbuf[...].astype(BF16)
     width = 512
     tiles_per = width // 128
+    low = lax.broadcasted_iota(jnp.int32, (tiles_per * pn, 128), 1) < 64
 
     @pl.loop(0, bs * bs // width)
     def _(j):
         r = jnp.dot(left, a_buf[:, pl.ds(pl.multiple_of(j * width, width), width)], preferred_element_type=F32)
-        for s in range(sig):
-            for t in range(tiles_per):
-                row0 = pl.multiple_of((s * half + j * tiles_per + t) * pn, 8)
-                zbuf[pl.ds(row0, pn), :] = r[s * pn:(s + 1) * pn, t * 128:(t + 1) * 128]
+        at = pl.ds(pl.multiple_of(j * tiles_per * pn, tiles_per * pn), tiles_per * pn)
+        for s in range(0, sig, 2):
+            z0, z1 = [jnp.concatenate(
+                [r[e * pn:(e + 1) * pn, t * 128:(t + 1) * 128] for t in range(tiles_per)], 0) for e in (s, s + 1)]
+            x0 = jnp.where(low, z0, pltpu.roll(z1, 64, 1))
+            x1 = jnp.where(low, pltpu.roll(z0, 64, 1), z1)
+            xbuf[0, at, s * bs:s * bs + 128] = x0.astype(BF16)
+            xbuf[1, at, s * bs:s * bs + 128] = x1.astype(BF16)
 
     for n, off in enumerate(offs):
         src = lax.rem(q + pairs - off, pairs)
@@ -164,36 +176,28 @@
         pltpu.make_async_remote_copy(
             src_ref=part, dst_ref=part, send_sem=msend.at[n], recv_sem=mrecv.at[n],
             device_id={"pair": q, "blk": sib}, device_id_type=MESH).wait_recv()
-        copy = to_sibling(core, src, n)
-        copy.start()
-        m_out.append(copy)
-
-    low = lax.broadcasted_iota(jnp.int32, (half, 128), 1) < 64
-
-    @pl.loop(0, pn)
-    def _(p):
-        for s in range(0, sig, 2):
-            z0 = zbuf[pl.ds(s * half * pn + p, half, stride=pn), :]
-            z1 = zbuf[pl.ds((s + 1) * half * pn + p, half, stride=pn), :]
-            x0 = jnp.where(low, z0, pltpu.roll(z1, 64, 1))
-            x1 = jnp.where(low, pltpu.roll(z0, 64, 1), z1)
-            at = pl.ds(pl.multiple_of(p * half, half), half)
-            xbuf[0, at, s * bs:s * bs + 128] = x0.astype(BF16)
-            xbuf[1, at, s * bs:s * bs + 128] = x1.astype(BF16)
-
-    met_t[core] = met_all[core].T
-    for n, off in enumerate(offs + [0]):
-        to_sibling(1 - core, lax.rem(q + pairs - off, pairs), n).wait_recv()
-    met_t[1 - core] = met_all[1 - core].T
-
-    block = 256
+
+    whole_half = [pltpu.make_async_remote_copy(
+        src_ref=met_all.at[h], dst_ref=met_all.at[h], send_sem=fsend.at[0], recv_sem=frecv.at[0],
+        device_id={"pair": q, "blk": sib}, device_id_type=MESH) for h in (core, 1 - core)]
+    whole_half[0].start()
+    m_out.append(whole_half[0])
+    xfirst = [jnp.dot(xbuf[h], perm[:, 0:768], preferred_element_type=F32).astype(BF16) for h in range(2)]
+    met_t[core] = jnp.dot(order[...], met_all[core], preferred_element_type=F32).astype(BF16).T
+    whole_half[1].wait_recv()
+    met_t[1 - core] = jnp.dot(order[...], met_all[1 - core], preferred_element_type=F32).astype(BF16).T
+
+    block = 768
     parts = cols // block
     y_out = []
     for c in range(parts):
         span = slice(c * block, (c + 1) * block)
         total = None
         for h in range(2):
-            xp = jnp.dot(xbuf[h], perm[:, span], preferred_element_type=F32).astype(BF16)
+            if c == 0:
+                xp = xfirst[h]
+            else:
+                xp = jnp.dot(xbuf[h], perm[:, span], preferred_element_type=F32).astype(BF16)
             term = jnp.dot(met_t[h], xp, preferred_element_type=F32)
             total = term if total is None else total + term
         ysend[c] = total.astype(BF16).reshape(pairs, bs, block)
@@ -230,7 +234,7 @@
         pn = aux // bs
         half = bs // 2
         n_off = pairs - 1
-        block = 256
+        block = 768
         parts = cols // block
         vmem = pl.BlockSpec(memory_space=pltpu.VMEM)
         smem = pl.BlockSpec(memory_space=pltpu.SMEM)
@@ -239,31 +243,33 @@
         return pl.pallas_call(
             functools.partial(kernel, pairs, blks),
             out_shape=pltpu.VMEM((pairs, 1, bs, cols), BF16),
-            in_specs=[smem, smem, smem, anyw, vmem, vmem],
+            in_specs=[smem, smem, smem, anyw, anyw, anyw],
             out_specs=vmem,
             scratch_shapes=[
                 pltpu.VMEM((groups * slots * bs, wide), BF16),
-                pltpu.VMEM((16, panel), BF16),
+                pltpu.VMEM((sig, panel), BF16),
+                pltpu.VMEM((bs, aux), BF16),
                 pltpu.VMEM((blks, 8, 128), jnp.int32),
                 pltpu.VMEM((blks, 8, 128), jnp.int32),
                 pltpu.VMEM((blks, 16, 128), BF16),
                 pltpu.VMEM((blks, 16, 128), BF16),
                 pltpu.VMEM((2, pn * half, aux), BF16),
                 pltpu.VMEM((2, aux, pn * half), BF16),
-                pltpu.VMEM((sig * half * pn, 128), F32),
+                pltpu.VMEM((pn * half, pn * half), BF16),
                 pltpu.VMEM((2, pn * half, cols), BF16),
                 pltpu.VMEM((cols, cols), BF16),
                 pltpu.VMEM((parts, pairs, bs, block), BF16),
                 pltpu.VMEM((sig * pn, groups * slots * bs), F32),
                 dma((groups * slots,)),
+                dma((2,)),
                 dma((blks,)),
                 dma((blks,)),
                 dma((blks,)),
                 dma((blks,)),
                 dma((n_off,)),
                 dma((n_off,)),
-                dma((n_off + 1,)),
-                dma((n_off + 1,)),
+                dma((1,)),
+                dma((1,)),
                 dma((parts, n_off)),
                 dma((parts, n_off)),
                 dma((parts,)),

time: 35.7 us -> 34.6 us (0.969)
  Pallas kernels: 34.6 us -> 33.5 us
    pallas_call x1, Pallas kernels: 34.6 us -> 33.5 us  [per_device(): pl.pallas_call(functools.partial(kernel, pairs, blks), out_shape=pltpu.VM...]
where the time goes in v3:
time: 34.6 us; the launch traced here: 34.4 us
  Pallas kernels  33.5 us (97%)
  local copies, waits for them, and re-layouts  0.88 us (3%)
    pallas_call x1, Pallas kernels, per_device(): pl.pallas_call(functools.partial(kernel, pairs, blks), out_shape=pltpu.VM...  33.5 us
    unnamed x1, local copies, waits for them, and re-layouts  0.88 us

profile of v3, /device:TPU:0, one launch (start us, length us, event | category | flops | bytes accessed | tf_op | source)
XLA Modules:
  0.0 34.4 jit_solution(7859538761431636549)
XLA Ops:
  0.0 33.5 %shard_map.64 = bf16[8,1,64,768]{3,2,1,0:T(8,128)(2,1)S(1)} custom-call(s32[1,2,4]{2,1,0:T(2,128)} %bitcast.2, s32[1,2,4]{2,1,0:T(2,128)} %bitcast.3, s32[1,4]{1,0:T(1,128)} %cnt_ref.1, bf16[1,4,2,64,4096]{4,3,2,1,0:T(8,128)(2,1)} %ints_ref.1, bf16[12,4096]{1,0:T(8,128)(2,1)} %dens_ref.1, bf16[64,512]{1,0:T(8,128)(2,1)} %metric_ref.1), custom_call_target="tpu_custom_call" | custom-call | flops 2000000000 | bytes 6000000 | tf_op jit(solution)/shard_map/pallas_call | solution.py:243
  33.5 0.9 %copy.8 = bf16[8,1,64,768]{3,2,1,0:T(8,128)(2,1)} copy(bf16[8,1,64,768]{3,2,1,0:T(8,128)(2,1)S(1)} %shard_map.64) | data formatting | bytes 1572864
